TPU v7x, 1024 devices: a whole 4x4x32 slice. The times are simulated.
1024 devices in a mesh: hi: 16 (over y_hi, x, core), lo: 64 (over y_lo, z).
Axes of the slice: x: 4, y: 4 (y_hi: 2, y_lo: 2; y = y_hi * 2 + y_lo), z: 32, core: 2. Of those that a mesh axis runs over, the one named last changes fastest.
Arguments:
- ket_state: float32 [2, 16777216], P(None, ('hi', 'lo')), may hold values from -6 to 6
- bra_state: float32 [2, 16777216], P(None, ('hi', 'lo')), may hold values from -6 to 6
- gate_matrices: float32 [5, 64, 128], replicated, may hold values from -0.5 to 0.5
Outputs:
- ket_out: float32 [2, 16777216], P(None, ('hi', 'lo'))
- bra_out: float32 [2, 16777216], P(None, ('hi', 'lo'))
- gradient: float32 [5, 64, 128], P(None, 'lo')
All inputs are finite; a program needn't handle non-finite values.
Results may differ from a plain program's by a relative error of at most 0.0001.
Values sent between devices are 32-bit elements; how exact they have to be, the bound alone decides.
A program may use at most 64 MiB of HBM per device.

v0:
```python
import jax
import jax.numpy as jnp
import numpy as np
from jax import lax
from jax.sharding import PartitionSpec as P

highest_precision = lax.Precision.HIGHEST


def from_partner(block, axis, apart):
    count = lax.axis_size(axis)
    route = []
    for low in range(count):
        high = low | 1 << apart
        if high != low and high < count:
            route += [(low, high), (high, low)]
    return lax.ppermute(block, axis, route)


def layer_bits(layer_index, local_bits):
    first_bits = [local_bits - 6, 0, local_bits // 2 - 3, 1, local_bits - 7]
    ordering = [2, 0, 5, 1, 4, 3]
    first_bit = first_bits[layer_index % 5]
    chosen = [(first_bit + ordering[(slot + layer_index) % 6]) % local_bits for slot in range(6)]
    if layer_index == 0:
        partner_bit = local_bits - 1
    elif layer_index == 1:
        partner_bit = 0
    else:
        partner_bit = (first_bit + 2) % local_bits
    return (first_bit, chosen, partner_bit)


def gate_order(first_bit, chosen, gate_size):
    mapping = np.zeros(gate_size, dtype=np.int64)
    for contiguous in range(gate_size):
        gate_index = 0
        for slot in range(6):
            offset = chosen[slot] - first_bit
            gate_index += (contiguous >> offset & 1) << slot
        mapping[contiguous] = gate_index
    inverse = np.argsort(mapping)
    both = np.concatenate([mapping, mapping + gate_size])
    both_inverse = np.concatenate([inverse, inverse + gate_size])
    return (both, both_inverse)


def conj_block(gate_matrix, gate_size):
    real_part = gate_matrix[:, :gate_size]
    imag_part = gate_matrix[:, gate_size:]
    return jnp.concatenate(
        [jnp.concatenate([real_part, -imag_part], 1), jnp.concatenate([imag_part, real_part], 1)], 0
    )


def undo_gate(state, unapply_four, low_size, gate_size):
    amplitudes = state.shape[1]
    high_size = amplitudes // (gate_size * low_size)
    if low_size <= 8:
        identity = jnp.eye(low_size, dtype=jnp.float32)
        widened = unapply_four[:, :, None, :, :, None] * identity[None, None, :, None, None, :]
        widened = widened.reshape(2, gate_size * low_size, 2, gate_size * low_size)
        flat = state.reshape(2, high_size, gate_size * low_size)
        result = jnp.einsum(
            "khx,kxjy->jhy",
            flat,
            widened,
            precision=highest_precision,
            preferred_element_type=jnp.float32,
        )
    else:
        shaped = state.reshape(2, high_size, gate_size, low_size)
        result = jnp.einsum(
            "khcl,kcjd->jhdl",
            shaped,
            unapply_four,
            precision=highest_precision,
            preferred_element_type=jnp.float32,
        )
    return result.reshape(2, amplitudes)


def outer_grad(bra_state, ket_state, low_size, gate_size, both_inverse):
    amplitudes = bra_state.shape[1]
    high_size = amplitudes // (gate_size * low_size)
    if low_size <= 8:
        bra_flat = bra_state.reshape(2, high_size, gate_size * low_size)
        ket_flat = ket_state.reshape(2, high_size, gate_size * low_size)
        wide = jnp.einsum(
            "khx,jhy->kxjy",
            bra_flat,
            ket_flat,
            precision=highest_precision,
            preferred_element_type=jnp.float32,
        )
        wide = wide.reshape(2, gate_size, low_size, 2, gate_size, low_size)
        product = jnp.einsum("kcljdl->kcjd", wide)
    else:
        bra_shaped = bra_state.reshape(2, high_size, gate_size, low_size)
        ket_shaped = ket_state.reshape(2, high_size, gate_size, low_size)
        product = jnp.einsum(
            "khcl,jhdl->kcjd",
            bra_shaped,
            ket_shaped,
            precision=highest_precision,
            preferred_element_type=jnp.float32,
        )
    product = product.reshape(2 * gate_size, 2 * gate_size)
    product = product[both_inverse][:, both_inverse]
    real_part = product[:gate_size, :gate_size] + product[gate_size:, gate_size:]
    imag_part = product[:gate_size, gate_size:] - product[gate_size:, :gate_size]
    return jnp.concatenate([real_part, imag_part], 1)


def picking_table(partner_bit, wanted):
    table = np.zeros((128, 64), dtype=np.float32)
    column = 0
    for position in range(128):
        if position >> partner_bit & 1 == wanted:
            table[position, column] = 1.0
            column += 1
    return table


def split_half(state, partner_bit, select):
    amplitudes = state.shape[1]
    if partner_bit < 7:
        table = jnp.where(
            select == 0,
            jnp.asarray(picking_table(partner_bit, 0)),
            jnp.asarray(picking_table(partner_bit, 1)),
        )
        shaped = state.reshape(2, amplitudes // 128, 128)
        half = jnp.einsum(
            "kni,im->knm",
            shaped,
            table,
            precision=highest_precision,
            preferred_element_type=jnp.float32,
        )
        return half.reshape(2, amplitudes // 2)
    shaped = state.reshape(2, amplitudes >> partner_bit + 1, 2, 1 << partner_bit)
    half = lax.dynamic_index_in_dim(shaped, select, 2, keepdims=False)
    return half.reshape(2, amplitudes // 2)


def place_half(state, arrived, partner_bit, select):
    amplitudes = state.shape[1]
    if partner_bit < 7:
        table = jnp.where(
            select == 0,
            jnp.asarray(picking_table(partner_bit, 0)),
            jnp.asarray(picking_table(partner_bit, 1)),
        )
        positions = np.arange(128)
        bit_values = jnp.asarray((positions >> partner_bit & 1).astype(np.int32))
        keep = (bit_values != select).astype(jnp.float32)
        shaped = state.reshape(2, amplitudes // 128, 128)
        incoming = arrived.reshape(2, amplitudes // 128, 64)
        spread = jnp.einsum(
            "knm,im->kni",
            incoming,
            table,
            precision=highest_precision,
            preferred_element_type=jnp.float32,
        )
        return (shaped * keep + spread).reshape(2, amplitudes)
    shaped = state.reshape(2, amplitudes >> partner_bit + 1, 2, 1 << partner_bit)
    incoming = arrived.reshape(2, amplitudes >> partner_bit + 1, 1, 1 << partner_bit)
    marked = (jnp.arange(2, dtype=jnp.int32) == select).reshape(1, 1, 2, 1)
    return jnp.where(marked, incoming, shaped).reshape(2, amplitudes)


def body(ket_state, bra_state, gate_matrices):
    amplitudes = ket_state.shape[1]
    gate_size = gate_matrices.shape[1]
    layer_count = gate_matrices.shape[0]
    local_bits = amplitudes.bit_length() - 1
    hi_bits = lax.axis_size("hi").bit_length() - 1
    lo_bits = lax.axis_size("lo").bit_length() - 1
    scale = (gate_size / (amplitudes * lax.axis_size("hi") * lax.axis_size("lo"))) ** 0.5
    reduced = [None] * layer_count
    for layer_index in reversed(range(layer_count)):
        first_bit, chosen, partner_bit = layer_bits(layer_index, local_bits)
        low_size = 1 << first_bit
        both, both_inverse = gate_order(first_bit, chosen, gate_size)
        unapply = conj_block(gate_matrices[layer_index], gate_size)
        unapply = unapply[both][:, both].reshape(2, gate_size, 2, gate_size)
        ket_state = undo_gate(ket_state, unapply, low_size, gate_size)
        on_high = layer_index % 2 == 0
        device_bit = layer_index // 2 % (hi_bits if on_high else lo_bits)
        own_index = lax.axis_index("hi") if on_high else lax.axis_index("lo")
        select = 1 - (jnp.right_shift(own_index, device_bit) & 1)
        term = outer_grad(bra_state, ket_state, low_size, gate_size, both_inverse)
        bra_state = undo_gate(bra_state, unapply, low_size, gate_size)
        ket_half = split_half(ket_state, partner_bit, select)
        bra_half = split_half(bra_state, partner_bit, select)
        if on_high:
            ket_back, bra_back = from_partner((ket_half, bra_half), "hi", device_bit)
        else:
            ket_back, bra_back = from_partner((ket_half, bra_half), "lo", device_bit)
        ket_state = place_half(ket_state, ket_back, partner_bit, select)
        bra_state = place_half(bra_state, bra_back, partner_bit, select)
        owned = lax.psum_scatter(term, "lo", scatter_dimension=0, tiled=True)
        reduced[layer_index] = lax.psum(owned, "hi") * scale
    gradient = jnp.stack(reduced)
    return (ket_state, bra_state, gradient)


def solution(mesh):
    placed = (P(None, ("hi", "lo")), P(None, ("hi", "lo")), P())
    return jax.shard_map(
        body,
        mesh=mesh,
        in_specs=placed,
        out_specs=(P(None, ("hi", "lo")), P(None, ("hi", "lo")), P(None, "lo", None)),
        check_vma=False,
    )
```

profile of v0, /device:TPU:1, one launch (start us, length us, event | category | flops | bytes accessed | tf_op | source)
XLA Modules:
  0.0 671.9 jit_solution(14110471736132710239)
XLA Ops:
  7.2 0.8 slice_bitcast_fusion.4
  8.1 0.9 copy.341
  9.1 0.7 pad_clamp_fusion.4
  9.8 0.6 gather_fusion.8
  10.6 0.7 gather_fusion.9
  12.0 5.5 collective-permute-start.5
  17.5 0.9 copy.336
  19.1 1.9 collective-permute-start
  21.1 0.7 pad_clamp_fusion.6
  21.9 0.6 gather_fusion.4
  22.6 0.6 gather_fusion.5
  23.6 0.6 gather_fusion.6
  24.4 0.7 gather_fusion.7
  25.4 6.6 broadcast_multiply_fusion
  32.0 12.6 %mul.103 = f32[2,128,2,128]{3,1,2,0:T(8,128)S(1)} reshape(f32[2,64,2,2,64,2]{5,4,2,1,3,0:T(8,128)} %broadcast_multiply_fusion) | data formatting | bytes 524288 | tf_op jit(solution)/shard_map/mul | solution.py:61
  44.8 0.6 gather_fusion.2
  45.6 0.7 gather_fusion.3
  46.6 0.6 gather_fusion
  47.3 0.6 gather_fusion.1
  49.0 0.6 gather_fusion.18
  49.8 0.7 gather_fusion.19
  50.5 0.6 pad_maximum_fusion.4
  51.2 1.3 dynamic-slice
  52.8 0.6 convolution_bitcast_fusion.2
  53.4 0.4 fusion.50
  53.9 5.1 collective-permute-start.6
  59.2 0.6 fusion.15
  59.8 0.4 fusion.13
  60.3 2.1 collective-permute-start.1
  62.7 0.6 fusion
  63.5 0.6 gather_fusion.16
  64.3 0.7 gather_fusion.17
  65.0 0.6 pad_maximum_fusion.3
  66.5 1.8 convolution_bitcast_fusion
  68.3 0.4 copy.244
  69.4 3.1 collective-permute-start.7
  73.4 1.8 fusion.2
  75.2 0.4 copy.225
  76.3 2.2 collective-permute-start.2
  79.4 0.4 convolution_bitcast_fusion.4
  79.7 0.6 gather_fusion.14
  80.5 0.6 gather_fusion.15
  81.2 0.6 pad_maximum_fusion.2
  82.4 0.4 convolution_bitcast_fusion.1
  83.4 3.5 collective-permute-start.8
  87.5 0.4 fusion.5
  88.5 1.9 collective-permute-start.3
  90.9 0.6 gather_fusion.12
  91.6 0.7 gather_fusion.13
  92.3 0.6 pad_maximum_fusion.1
  94.0 16.9 %collective-permute-start.9 = (f32[2,8192]{1,0:T(2,128)S(1)}, f32[2,8192]{1,0:T(2,128)S(1)}, u32[]{:S(2)}, u32[]{:S(2)}) collective-permute-start(f32[2,8192]{1,0:T(2,128)S(1)} %bitcast.307), channel_id=1, source_target_pairs={{0,64},{64,0},{128,192},{192,128},{256,320},{320,256},{384,448},{4... | collective-permute-start | bytes 196616 | tf_op jit(solution)/shard_map/ppermute | solution.py:17
  112.0 1.9 collective-permute-start.4
  114.3 0.6 gather_fusion.10
  115.1 0.7 gather_fusion.11
  115.8 0.6 pad_maximum_fusion
  116.8 0.9 broadcast_select_fusion.2
  117.7 431.1 %all-reduce.9.cloned.1.call-done = (f32[64,128]{0,1:T(8,128)}, f32[64,128]{0,1:T(8,128)}, f32[64,128]{0,1:T(8,128)}, f32[64,128]{0,1:T(8,128)}, f32[64,128]{0,1:T(8,128)}) async-done(((f32[64,128]{0,1:T(8,128)}, f32[64,128]{0,1:T(8,128)}, f32[64,128]{0,1:T(8,128)}, f32[64,128]{0,1:T(8,128)}, f32[64,128]{0,1:T(8,128)}), (f32[64,128]{0,1:T(8,128)}, f32[64,128]{0,1:T(8,128)}, f32[64,128]{0,1:T(8,128)}, ...) | async-done | bytes 163856
  548.9 1.6 constant_dynamic-slice_fusion.4
  550.4 1.6 constant_dynamic-slice_fusion.3
  552.0 1.6 constant_dynamic-slice_fusion.2
  553.6 1.6 constant_dynamic-slice_fusion.1
  555.1 1.6 constant_dynamic-slice_fusion
  556.7 107.1 %all-reduce.6 = (f32[1,128]{0,1:T(8,128)S(1)}, f32[1,128]{0,1:T(8,128)S(1)}, f32[1,128]{0,1:T(8,128)S(1)}, f32[1,128]{0,1:T(8,128)S(1)}, f32[1,128]{0,1:T(8,128)S(1)}) all-reduce(f32[1,128]{0,1:T(8,128)S(1)} %constant_dynamic-slice_fusion.4, f32[1,128]{0,1:T(8,128)S(1)} %constant_dynamic-slice_fusion.3, ...), channel_id=1, replica_groups=mesh['hi'=16,'lo'=64] {'hi'}, use_global_device_ids=true, to_apply=%region_1.2 | all-reduce | flops 640 | bytes 5120 | tf_op jit(solution)/shard_map/psum | solution.py:205
  664.5 0.6 copy-done.14
  (175 shorter events, 16.2 us)
Async XLA Ops:
  7.2 541.7 %all-reduce.9.cloned.1.call-start = ((), (), s32[]{:S(2)}) async-start(), calls=%async_computation | async-start | bytes 655360
  12.0 40.4 %collective-permute-start.5 = (f32[2,8192]{1,0:T(2,128)S(1)}, f32[2,8192]{1,0:T(2,128)S(1)}, u32[]{:S(2)}, u32[]{:S(2)}) collective-permute-start(f32[2,8192]{1,0:T(2,128)S(1)} %bitcast.303), channel_id=1, source_target_pairs={{0,256},{256,0},{64,320},{320,64},{128,384},{384,128},{192,448},{4... | collective-permute-start | bytes 196616 | tf_op jit(solution)/shard_map/ppermute | solution.py:17
  19.1 33.4 %collective-permute-start = (f32[2,8192]{1,0:T(2,128)S(1)}, f32[2,8192]{1,0:T(2,128)S(1)}, u32[]{:S(2)}, u32[]{:S(2)}) collective-permute-start(f32[2,8192]{1,0:T(2,128)S(1)} %bitcast.305), channel_id=1, source_target_pairs={{0,256},{256,0},{64,320},{320,64},{128,384},{384,128},{192,448},{4... | collective-permute-start | bytes 196616 | tf_op jit(solution)/shard_map/ppermute | solution.py:17
  25.3 19.4 %copy-start.13 = (s32[128]{0:T(128)S(1)}, s32[128]{0:T(128)}, u32[]{:S(2)}) copy-start(s32[128]{0:T(128)} %constant.82.clone) | copy-start | bytes 1540
  25.3 19.4 %copy-start.12 = (s32[128]{0:T(128)S(1)}, s32[128]{0:T(128)}, u32[]{:S(2)}) copy-start(s32[128]{0:T(128)} %constant.86.clone) | copy-start | bytes 1540
  25.3 21.1 %copy-start.11 = (s32[128]{0:T(128)S(1)}, s32[128]{0:T(128)}, u32[]{:S(2)}) copy-start(s32[128]{0:T(128)} %constant.91.clone) | copy-start | bytes 1540
  25.3 21.2 %copy-start.10 = (s32[128]{0:T(128)S(1)}, s32[128]{0:T(128)}, u32[]{:S(2)}) copy-start(s32[128]{0:T(128)} %constant.103) | copy-start | bytes 1540
  25.3 23.7 %copy-start.8 = (s32[128]{0:T(128)S(1)}, s32[128]{0:T(128)}, u32[]{:S(2)}) copy-start(s32[128]{0:T(128)} %constant.121) | copy-start | bytes 1540
  25.3 23.7 %copy-start.9 = (s32[128]{0:T(128)S(1)}, s32[128]{0:T(128)}, u32[]{:S(2)}) copy-start(s32[128]{0:T(128)} %constant.119) | copy-start | bytes 1540
  25.4 25.2 %copy-start.6 = (s32[128]{0:T(128)S(1)}, s32[128]{0:T(128)}, u32[]{:S(2)}) copy-start(s32[128]{0:T(128)} %constant.115) | copy-start | bytes 1540
  25.4 25.2 %copy-start.7 = (s32[128]{0:T(128)S(1)}, s32[128]{0:T(128)}, u32[]{:S(2)}) copy-start(s32[128]{0:T(128)} %constant.113) | copy-start | bytes 1540
  25.4 28.0 %copy-start.4 = (f32[128,64]{0,1:T(8,128)S(1)}, f32[128,64]{0,1:T(8,128)}, u32[]{:S(2)}) copy-start(f32[128,64]{0,1:T(8,128)} %constant.80.clone) | copy-start | bytes 98308
  25.4 28.0 %copy-start.5 = (f32[128,64]{0,1:T(8,128)S(1)}, f32[128,64]{0,1:T(8,128)}, u32[]{:S(2)}) copy-start(f32[128,64]{0,1:T(8,128)} %constant.81.clone) | copy-start | bytes 98308
  32.0 37.0 %copy-start.2 = (f32[128,64]{0,1:T(8,128)S(1)}, f32[128,64]{0,1:T(8,128)}, u32[]{:S(2)}) copy-start(f32[128,64]{0,1:T(8,128)} %constant.84.clone) | copy-start | bytes 98308
  32.0 37.0 %copy-start.3 = (f32[128,64]{0,1:T(8,128)S(1)}, f32[128,64]{0,1:T(8,128)}, u32[]{:S(2)}) copy-start(f32[128,64]{0,1:T(8,128)} %constant.85.clone) | copy-start | bytes 98308
  44.8 38.2 %copy-start = (f32[128,64]{0,1:T(8,128)S(1)}, f32[128,64]{0,1:T(8,128)}, u32[]{:S(2)}) copy-start(f32[128,64]{0,1:T(8,128)} %constant.89.clone) | copy-start | bytes 98308
  44.8 38.2 %copy-start.1 = (f32[128,64]{0,1:T(8,128)S(1)}, f32[128,64]{0,1:T(8,128)}, u32[]{:S(2)}) copy-start(f32[128,64]{0,1:T(8,128)} %constant.90.clone) | copy-start | bytes 98308
  53.9 11.7 %collective-permute-start.6 = (f32[2,8192]{1,0:T(2,128)S(1)}, f32[2,8192]{1,0:T(2,128)S(1)}, u32[]{:S(2)}, u32[]{:S(2)}) collective-permute-start(f32[2,8192]{1,0:T(2,128)S(1)} %reshape.275), channel_id=1, source_target_pairs={{0,2},{2,0},{1,3},{3,1},{4,6},{6,4},{5,7},{7,5},{8,10},{10,8},{9,1... | collective-permute-start | bytes 196616 | tf_op jit(solution)/shard_map/ppermute | solution.py:17
  60.3 12.2 %collective-permute-start.1 = (f32[2,8192]{1,0:T(2,128)S(1)}, f32[2,8192]{1,0:T(2,128)S(1)}, u32[]{:S(2)}, u32[]{:S(2)}) collective-permute-start(f32[2,8192]{1,0:T(2,128)S(1)} %reshape.265), channel_id=1, source_target_pairs={{0,2},{2,0},{1,3},{3,1},{4,6},{6,4},{5,7},{7,5},{8,10},{10,8},{9,1... | collective-permute-start | bytes 196616 | tf_op jit(solution)/shard_map/ppermute | solution.py:17
  69.4 12.5 %collective-permute-start.7 = (f32[2,8192]{1,0:T(2,128)S(1)}, f32[2,8192]{1,0:T(2,128)S(1)}, u32[]{:S(2)}, u32[]{:S(2)}) collective-permute-start(f32[2,8192]{1,0:T(2,128)S(1)} %reshape.277), channel_id=1, source_target_pairs={{0,128},{128,0},{64,192},{192,64},{256,384},{384,256},{320,448},{4... | collective-permute-start | bytes 196616 | tf_op jit(solution)/shard_map/ppermute | solution.py:17
  76.3 10.7 %collective-permute-start.2 = (f32[2,8192]{1,0:T(2,128)S(1)}, f32[2,8192]{1,0:T(2,128)S(1)}, u32[]{:S(2)}, u32[]{:S(2)}) collective-permute-start(f32[2,8192]{1,0:T(2,128)S(1)} %reshape.267), channel_id=1, source_target_pairs={{0,128},{128,0},{64,192},{192,64},{256,384},{384,256},{320,448},{4... | collective-permute-start | bytes 196616 | tf_op jit(solution)/shard_map/ppermute | solution.py:17
  83.4 9.6 %collective-permute-start.8 = (f32[2,8192]{1,0:T(2,128)S(1)}, f32[2,8192]{1,0:T(2,128)S(1)}, u32[]{:S(2)}, u32[]{:S(2)}) collective-permute-start(f32[2,8192]{1,0:T(2,128)S(1)} %reshape.279), channel_id=1, source_target_pairs={{0,1},{1,0},{2,3},{3,2},{4,5},{5,4},{6,7},{7,6},{8,9},{9,8},{10,11... | collective-permute-start | bytes 196616 | tf_op jit(solution)/shard_map/ppermute | solution.py:17
  88.5 22.5 %collective-permute-start.3 = (f32[2,8192]{1,0:T(2,128)S(1)}, f32[2,8192]{1,0:T(2,128)S(1)}, u32[]{:S(2)}, u32[]{:S(2)}) collective-permute-start(f32[2,8192]{1,0:T(2,128)S(1)} %reshape.269), channel_id=1, source_target_pairs={{0,1},{1,0},{2,3},{3,2},{4,5},{5,4},{6,7},{7,6},{8,9},{9,8},{10,11... | collective-permute-start | bytes 196616 | tf_op jit(solution)/shard_map/ppermute | solution.py:17
  94.0 22.5 %collective-permute-start.9 = (f32[2,8192]{1,0:T(2,128)S(1)}, f32[2,8192]{1,0:T(2,128)S(1)}, u32[]{:S(2)}, u32[]{:S(2)}) collective-permute-start(f32[2,8192]{1,0:T(2,128)S(1)} %bitcast.307), channel_id=1, source_target_pairs={{0,64},{64,0},{128,192},{192,128},{256,320},{320,256},{384,448},{4... | collective-permute-start | bytes 196616 | tf_op jit(solution)/shard_map/ppermute | solution.py:17
  112.0 4.6 collective-permute-start.4
  664.5 0.6 copy-start.14
Sparse Core Ops, SparseCore 0:
  116.6 432.2 all-reduce.8
where the time goes:
time: 678 us; the launch traced here: 672 us
  waiting for transfers between devices  431 us (64%)
  blocking collectives  107 us (16%)
  local copies, waits for them, and re-layouts  48 us (7%)
  starting transfers between devices  44.2 us (7%)
  between operations  15.4 us (2%)
  other arithmetic  13.9 us (2%)
  matrix products  12.1 us (2%)
    unnamed x2, waiting for transfers between devices  431 us
    psum x1, blocking collectives, body(): reduced[layer_index] = lax.psum(owned, 'hi') * scale  107 us
    ppermute x10, starting transfers between devices, from_partner(): return lax.ppermute(block, axis, route)  44.2 us
  transfers between devices with their start and end apart: 11, of which 1 were waited for; matrix products, arithmetic and copies ran while one was open for 9% of the time, Pallas kernels for 0%

commit v1 on v0

v1 whole, which is shorter than its diff:
```python
import functools

import jax
import jax.numpy as jnp
from jax import lax
from jax.experimental import pallas as pl
from jax.experimental.pallas import tpu as pltpu
from jax.sharding import PartitionSpec as P

F32 = jnp.float32
BF16 = jnp.bfloat16
MESH = pl.DeviceIdType.MESH
LOCAL_BITS = 14
FIRST = (8, 0, 4, 1, 7)
ORDER = (2, 0, 5, 1, 4, 3)
ROWS = (7, 8, 13, 10, 11, 12, 9)
LANES = (0, 1, 2, 3, 4, 5, 6)
ROWS_MIXED = (7, 8, 13, 4, 5, 6, 9)
NN = (((1,), (0,)), ((), ()))
NT = (((1,), (1,)), ((), ()))
TN = (((0,), (0,)), ((), ()))


def target_bits(layer):
    return [(FIRST[layer] + ORDER[(j + layer) % 6]) % LOCAL_BITS for j in range(6)]


def mm(a, b, dims):
    return lax.dot_general(a, b, dims, preferred_element_type=F32)


def halves(x):
    top = x.astype(BF16)
    return top, (x - top.astype(F32)).astype(BF16)


def mm3(a, b, dims):
    return mm(a[0], b[0], dims) + mm(a[0], b[1], dims) + mm(a[1], b[0], dims)


def gate_code(index, layer, bits):
    code = None
    for j, target in enumerate(target_bits(layer)):
        term = ((index >> bits.index(target)) & 1) << j
        code = term if code is None else code + term
    return code


def rest_position(layer, bits):
    targets = target_bits(layer)
    return [i for i, bit in enumerate(bits) if bit not in targets][0]


def picks(layer, bits):
    row = lax.broadcasted_iota(jnp.int32, (256, 128), 0)
    column = lax.broadcasted_iota(jnp.int32, (256, 128), 1)
    code = gate_code(row & 127, layer, bits) + ((row >> 7) << 6)
    return (code == column).astype(F32).astype(BF16)


def rest_mask(layer, bits):
    i = lax.broadcasted_iota(jnp.int32, (128, 128), 0)
    j = lax.broadcasted_iota(jnp.int32, (128, 128), 1)
    return (((i ^ j) >> rest_position(layer, bits)) & 1) == 0


def spread_gate(u, layer, bits, picked, mask, on_rows):
    row = lax.broadcasted_iota(jnp.int32, (128, 64), 0)
    column = lax.broadcasted_iota(jnp.int32, (128, 64), 1)
    chooser = (gate_code(row, layer, bits) == column).astype(F32).astype(BF16)
    u_parts = halves(u)
    tall = jnp.concatenate([mm(chooser, part, NN).astype(BF16) for part in u_parts], 0)
    out = []
    if on_rows:
        wide = mm(picked, tall, NT)
        for part in range(2):
            columns = slice(128 * part, 128 * part + 128)
            real = jnp.where(mask, wide[:128, columns], 0.0)
            imag = jnp.where(mask, wide[128:, columns], 0.0)
            out.append(jnp.concatenate([jnp.concatenate([real, imag], 1), jnp.concatenate([-imag, real], 1)], 0).astype(BF16))
    else:
        wide = mm(tall, picked, NT)
        for part in range(2):
            rows = slice(128 * part, 128 * part + 128)
            real = jnp.where(mask, wide[rows, :128], 0.0)
            imag = jnp.where(mask, wide[rows, 128:], 0.0)
            out.append(jnp.concatenate([jnp.concatenate([real, -imag], 1), jnp.concatenate([imag, real], 1)], 0).astype(BF16))
    return tuple(out)


def undo_on_rows(gate, x):
    flat = jnp.concatenate([jnp.concatenate([x[0], x[2]], 1), jnp.concatenate([x[1], x[3]], 1)], 0)
    y = mm3(gate, halves(flat), NN)
    return [y[:128, :128], y[128:, :128], y[:128, 128:], y[128:, 128:]]


def undo_on_lanes(gate, x):
    flat = jnp.concatenate([jnp.concatenate([x[0], x[1]], 1), jnp.concatenate([x[2], x[3]], 1)], 0)
    y = mm3(halves(flat), gate, NN)
    return [y[:128, :128], y[:128, 128:], y[128:, :128], y[128:, 128:]]


def outer_on_rows(bra, ket):
    left = jnp.concatenate(bra, 1)
    right = jnp.concatenate([jnp.concatenate([ket[0], ket[1]], 1), jnp.concatenate([ket[1], -ket[0]], 1)], 0)
    return mm3(halves(left), halves(right), NT)


def outer_on_lanes(bra, ket):
    left = jnp.concatenate(bra, 0)
    right = jnp.concatenate([jnp.concatenate([ket[0], ket[1]], 1), jnp.concatenate([ket[1], -ket[0]], 1)], 0)
    return mm3(halves(left), halves(right), TN)


def to_chunks(wide, layer, bits, picked, mask, slot):
    kept = jnp.concatenate([jnp.where(mask, wide[:, :128], 0.0), jnp.where(mask, wide[:, 128:], 0.0)], 1)
    both = mm(jnp.concatenate(halves(kept), 0), picked, NN)
    narrow = jnp.concatenate(halves(both[:128] + both[128:]), 0)
    row = lax.broadcasted_iota(jnp.int32, (256, 256), 0)
    column = lax.broadcasted_iota(jnp.int32, (256, 256), 1)
    code = gate_code(column & 127, layer, bits)
    place = ((code & 15) << 4) + ((code >> 5) << 3) + (((code >> 4) & 1) << 2) + slot
    return mm((row == place).astype(F32).astype(BF16), narrow, NN)


def swap_lane(x, row_bit, lane_bit):
    size, step = 1 << row_bit, 1 << lane_bit
    lane = lax.broadcasted_iota(jnp.int32, (size, 128), 1)
    upper = ((lane >> lane_bit) & 1) == 1
    out = []
    for base in range(0, 128, 2 * size):
        a, b = x[base : base + size], x[base + size : base + 2 * size]
        out.append(jnp.where(upper, pltpu.roll(b, step, 1), a))
        out.append(jnp.where(upper, b, pltpu.roll(a, 128 - step, 1)))
    return jnp.concatenate(out, 0)


def swap_sublane(x, row_bit):
    upper = lax.broadcasted_iota(jnp.int32, (8, 128), 0) >= 4
    tiles = [x[8 * i : 8 * i + 8] for i in range(16)]
    bit = 1 << (row_bit - 3)
    out = [None] * 16
    for i in range(16):
        if not i & bit:
            a, b = tiles[i], tiles[i | bit]
            out[i] = jnp.where(upper, pltpu.roll(b, 4, 0), a)
            out[i | bit] = jnp.where(upper, b, pltpu.roll(a, 4, 0))
    return jnp.concatenate(out, 0)


def kernel(
    scale, ket_ref, bra_ref, gate_ref, ket_out, bra_out, grad_out,
    send_a, recv_a, send_b, recv_b, chunks, partial, packed, column, final,
    a_send, a_recv, b_send, b_recv, c_send, c_recv, z_send, z_recv, f_send, f_recv, near, far,
):
    hi, lo = lax.axis_index("hi"), lax.axis_index("lo")
    z, y = lo & 31, lo >> 5

    def ring(step):
        return (hi, (lo & 32) + ((z + step) & 31))

    barrier = pltpu.get_barrier_semaphore()

    def greet(device):
        pl.semaphore_signal(barrier, inc=1, device_id=device, device_id_type=MESH)

    greet((hi ^ 4, lo ^ 2))
    for k in (1, 2, 3):
        greet((hi ^ k, lo ^ 1))
    for step in (1, 2, 3, 4):
        greet(ring(step))
        greet(ring(-step))

    me = hi * 2 + y

    def greet_plane(k, carry):
        other = me ^ k
        greet((other >> 1, (other & 1) * 32 + z))
        return carry

    lax.fori_loop(1, 32, greet_plane, 0)

    def layer_setup(layer, bits, on_rows):
        picked, mask = picks(layer, bits), rest_mask(layer, bits)
        return picked, mask, spread_gate(gate_ref[layer], layer, bits, picked, mask, on_rows)

    pick4, mask4, gate4 = layer_setup(4, ROWS, True)
    pick3, mask3, gate3 = layer_setup(3, LANES, False)

    x5 = [swap_sublane(r[i], 6) for r in (ket_ref, bra_ref) for i in range(2)]
    x4 = undo_on_rows(gate4, x5)
    x3 = undo_on_lanes(gate3, x4)
    mine = ((hi >> 2) & 1) * 2 + ((lo >> 1) & 1)
    for i in range(4):
        ready = swap_lane(x3[i], 5, 3)
        for block in range(4):
            send_a[block, i] = ready[32 * block : 32 * block + 32]
    recv_a[mine] = send_a[mine]

    pl.semaphore_wait(barrier, 43)

    copies_a = []
    for d in (3, 1, 2):
        copy = pltpu.make_async_remote_copy(
            send_a.at[mine ^ d], recv_a.at[mine], a_send.at[d], a_recv.at[d],
            device_id=(hi ^ (4 if d & 2 else 0), lo ^ (2 if d & 1 else 0)), device_id_type=MESH,
        )
        copy.start()
        copies_a.append(copy)
    for step in (4, -4):
        pl.semaphore_signal(near, inc=1, device_id=ring(step), device_id_type=MESH)

    def plane_copy(batch, k):
        other = me ^ k
        return pltpu.make_async_remote_copy(
            chunks.at[batch, other], partial.at[batch, me], c_send.at[batch, k], c_recv.at[batch, k],
            device_id=(other >> 1, (other & 1) * 32 + z), device_id_type=MESH,
        )

    def send_plane(batch, value):
        chunks[batch] = value.reshape(32, 8, 128)
        partial[batch, me] = chunks[batch, me]

        def go(k, carry):
            plane_copy(batch, k).start()
            return carry

        lax.fori_loop(1, 32, go, 0)

    def wait_plane(batch):
        def go(k, carry):
            plane_copy(batch, k).wait()
            return carry

        lax.fori_loop(1, 32, go, 0)
        return jnp.sum(partial[batch], 0)

    first = to_chunks(outer_on_rows(x5[2:], x4[:2]), 4, ROWS, pick4, mask4, 0)
    first += to_chunks(outer_on_lanes(x4[2:], x3[:2]), 3, LANES, pick3, mask3, 3)
    send_plane(0, first)

    pick2, mask2, gate2 = layer_setup(2, ROWS_MIXED, True)
    pick1, mask1, gate1 = layer_setup(1, LANES, False)
    pick0, mask0, gate0 = layer_setup(0, ROWS, True)
    pl.semaphore_wait(near, 2)
    for step in (8, -8):
        pl.semaphore_signal(far, inc=1, device_id=ring(step), device_id_type=MESH)

    for copy in copies_a:
        copy.wait()
    x = [jnp.concatenate([recv_a[block, i] for block in range(4)], 0) for i in range(4)]
    x = [swap_lane(v, 5, 3) for v in x]
    mixed = [swap_lane(swap_lane(swap_lane(v, 3, 4), 4, 5), 5, 6) for v in x]
    x2 = undo_on_rows(gate2, mixed)
    turned = [swap_lane(swap_lane(swap_lane(v, 3, 4), 4, 5), 5, 6) for v in x2]
    x1 = undo_on_lanes(gate1, turned)
    x0 = undo_on_rows(gate0, x1)

    second = to_chunks(outer_on_rows(x1[2:], x0[:2]), 0, ROWS, pick0, mask0, 0)
    second += to_chunks(outer_on_lanes(turned[2:], x1[:2]), 1, LANES, pick1, mask1, 1)
    second += to_chunks(outer_on_rows(mixed[2:], x2[:2]), 2, ROWS_MIXED, pick2, mask2, 2)
    send_plane(1, second)

    own = ((hi >> 1) & 1) * 4 + (lo & 1) * 2 + (hi & 1)
    for i in range(4):
        ready = swap_sublane(swap_lane(swap_lane(x0[i], 5, 6), 4, 0), 3)
        for block in range(8):
            for top in range(2):
                send_b[block, i, top] = ready[64 * top + 8 * block : 64 * top + 8 * block + 8]
    recv_b[own] = send_b[own]
    copies_b = []
    for d in range(1, 8):
        copy = pltpu.make_async_remote_copy(
            send_b.at[own ^ d], recv_b.at[own], b_send.at[d], b_recv.at[d],
            device_id=(hi ^ ((2 if d & 4 else 0) + (d & 1)), lo ^ (1 if d & 2 else 0)), device_id_type=MESH,
        )
        copy.start()
        copies_b.append(copy)

    sum1 = wait_plane(0)
    sum2 = wait_plane(1)
    sub = lax.broadcasted_iota(jnp.int32, (8, 128), 0)
    for q in range(2):
        late, early = (pltpu.roll(sum2, 4, 0), pltpu.roll(sum1, 4, 0)) if q else (sum2, sum1)
        other = sum1 if q else pltpu.roll(sum1, 4, 0)
        packed[q] = jnp.where(sub < 3, late, jnp.where(sub == 3, early, other))
    pl.semaphore_wait(far, 2)

    def column_copy(q):
        return pltpu.make_async_remote_copy(
            packed.at[q], column.at[z], z_send.at[q], z_recv.at[z],
            device_id=(hi, (lo & 32) + hi + 16 * q), device_id_type=MESH,
        )

    for q in range(2):
        @pl.when(z != hi + 16 * q)
        def _():
            column_copy(q).start()

        @pl.when(z == hi + 16 * q)
        def _():
            column[z] = packed[q]

    for copy in copies_b:
        copy.wait()
    for i in range(4):
        v = jnp.concatenate([recv_b[block, i, top] for top in range(2) for block in range(8)], 0)
        v = swap_lane(swap_lane(swap_sublane(v, 3), 4, 0), 5, 6)
        (ket_out, bra_out)[i // 2][i % 2] = swap_sublane(v, 6)

    for q in range(2):
        @pl.when(z != hi + 16 * q)
        def _():
            column_copy(q).wait_send()

    owner = (z & 15) == hi

    def final_copy(k, slot):
        return pltpu.make_async_remote_copy(
            final, final, f_send.at[k], f_recv, device_id=(hi ^ k, lo), device_id_type=MESH,
        )

    @pl.when(owner)
    def _():
        def arrive(source, carry):
            @pl.when(source != z)
            def _():
                pltpu.make_async_remote_copy(
                    packed.at[0], column.at[source], z_send.at[0], z_recv.at[source],
                    device_id=(hi, lo), device_id_type=MESH,
                ).wait_recv()

            return carry

        lax.fori_loop(0, 32, arrive, 0)
        final[...] = jnp.sum(column[...], 0) * scale

        def give(k, carry):
            final_copy(k, 0).start()
            return carry

        def given(k, carry):
            final_copy(k, 0).wait_send()
            return carry

        lax.fori_loop(1, 16, give, 0)
        lax.fori_loop(1, 16, given, 0)

    @pl.when(jnp.logical_not(owner))
    def _():
        final_copy(0, 0).wait_recv()

    grad_out[...] = final[...]


def body(ket_state, bra_state, gate_matrices):
    scale = (64 / (16384 * lax.axis_size("hi") * lax.axis_size("lo"))) ** 0.5
    vmem = pl.BlockSpec(memory_space=pltpu.VMEM)
    state = jax.ShapeDtypeStruct((2, 128, 128), F32)
    dma = pltpu.SemaphoreType.DMA
    ket, bra, grad = pl.pallas_call(
        functools.partial(kernel, scale),
        out_shape=(state, state, jax.ShapeDtypeStruct((8, 128), F32)),
        in_specs=[vmem] * 3,
        out_specs=(vmem,) * 3,
        scratch_shapes=[
            pltpu.VMEM((4, 4, 32, 128), F32),
            pltpu.VMEM((4, 4, 32, 128), F32),
            pltpu.VMEM((8, 4, 2, 8, 128), F32),
            pltpu.VMEM((8, 4, 2, 8, 128), F32),
            pltpu.VMEM((2, 32, 8, 128), F32),
            pltpu.VMEM((2, 32, 8, 128), F32),
            pltpu.VMEM((2, 8, 128), F32),
            pltpu.VMEM((32, 8, 128), F32),
            pltpu.VMEM((8, 128), F32),
            dma((4,)), dma((4,)), dma((8,)), dma((8,)),
            dma((2, 32)), dma((2, 32)), dma((2,)), dma((32,)), dma((16,)), dma,
            pltpu.SemaphoreType.REGULAR, pltpu.SemaphoreType.REGULAR,
        ],
        compiler_params=pltpu.CompilerParams(collective_id=0, has_side_effects=True, vmem_limit_bytes=40 * 2**20),
        name="window",
    )(ket_state.reshape(2, 128, 128), bra_state.reshape(2, 128, 128), gate_matrices)
    amplitudes = ket_state.shape[1]
    return ket.reshape(2, amplitudes), bra.reshape(2, amplitudes), grad[:5].reshape(5, 1, 128)


def solution(mesh):
    placed = (P(None, ("hi", "lo")), P(None, ("hi", "lo")), P())
    return jax.shard_map(
        body,
        mesh=mesh,
        in_specs=placed,
        out_specs=(P(None, ("hi", "lo")), P(None, ("hi", "lo")), P(None, "lo", None)),
        check_vma=False,
    )
```

time: 678 us -> 60.2 us (0.09)
  waiting for transfers between devices: 431 us -> 0 us
  blocking collectives: 107 us -> 0 us
  Pallas kernels: 0 us -> 55.9 us
  local copies, waits for them, and re-layouts: 48 us -> 3.13 us
  starting transfers between devices: 44.2 us -> 0 us
  between operations: 15.4 us -> 0.66 us
  other arithmetic: 13.9 us -> 0 us
  matrix products: 12.1 us -> 0 us
    unnamed x2 -> x0, waiting for transfers between devices: 431 us -> none
    psum x1 -> x0, blocking collectives: 107 us -> none  [body(): reduced[layer_index] = lax.psum(owned, 'hi') * scale]
    pallas_call x0 -> x1, Pallas kernels: none -> 55.9 us  [body(): pl.pallas_call(functools.partial(kernel, scale), out_shape=(state, state,...]
    ppermute x10 -> x0, starting transfers between devices: 44.2 us -> none  [from_partner(): return lax.ppermute(block, axis, route)]
    gather x30 -> x0, local copies, waits for them, and re-layouts: 13.8 us -> none  [the longest x15 6.92 us: body(): unapply = unapply[both][:, both].reshape(2, gate_size, 2, gate_size)]
    mul x3 -> x0, local copies, waits for them, and re-layouts: 12.9 us -> none  [undo_gate(): unapply_four[:, :, None, :, :, None]]
    dot_general x27 -> x0, matrix products: 12.1 us -> none  [the longest x6 4.79 us: undo_gate(): jnp.einsum('khcl,kcjd->jhdl', shaped, unapply_four, precision=highest_pre...]
    unnamed x54 -> x5, local copies, waits for them, and re-layouts: 12.4 us -> 2.11 us
  transfers between devices with their start and end apart: 11 -> 0, of which waited for: 1 -> 0; matrix products, arithmetic and copies ran while one was open for 9% -> 0% of each run, Pallas kernels for 0% -> 0%
where the time goes in v1:
time: 60.2 us; the launch traced here: 59.7 us
  Pallas kernels  55.9 us (93%)
  local copies, waits for them, and re-layouts  3.13 us (5%)
  between operations  0.66 us (1%)
    pallas_call x1, Pallas kernels, body(): pl.pallas_call(functools.partial(kernel, scale), out_shape=(state, state,...  55.9 us
    unnamed x5, local copies, waits for them, and re-layouts  2.11 us

profile of v1, /device:TPU:1, one launch (start us, length us, event | category | flops | bytes accessed | tf_op | source)
XLA Modules:
  0.0 59.7 jit_solution(1083175926749868198)
XLA Ops:
  0.6 0.0 copy-start
  0.6 1.0 %copy_bitcast_fusion.2 = (f32[2,128,128]{2,1,0:T(8,128)S(1)}, f32[2,128,128]{2,1,0:T(8,128)S(1)}) fusion(f32[1,2,128,128]{3,1,2,0:T(2,128)} %bitcast.20, f32[1,2,128,128]{3,1,2,0:T(2,128)} %bitcast.21), kind=kLoop, calls=%fused_computation.2 | loop fusion | bytes 524288 | tf_op jit(solution)/shard_map/reshape | solution.py:382
  1.7 0.0 copy-done
  1.7 55.9 %window.1 = (f32[2,128,128]{2,1,0:T(8,128)S(1)}, f32[2,128,128]{2,1,0:T(8,128)S(1)}, f32[8,128]{1,0:T(8,128)S(1)}) custom-call(f32[2,128,128]{2,1,0:T(8,128)S(1)} %get-tuple-element.13.ket_ref, f32[2,128,128]{2,1,0:T(8,128)S(1)} %get-tuple-element.12.bra_ref, f32[5,64,128]{2,1,0:T(8,128)S(1)} %copy-done), custom_call_target="tpu_custom_call" | custom-call | tf_op jit(solution)/shard_map/window/pallas_call | solution.py:361
  57.6 0.8 %copy.16 = f32[1,2,128,128]{3,1,2,0:T(2,128)} copy(f32[1,2,128,128]{3,2,1,0:T(8,128)S(1)} %bitcast.17) | data formatting | bytes 262144
  58.3 0.8 %copy.15 = f32[1,2,128,128]{3,1,2,0:T(2,128)} copy(f32[1,2,128,128]{3,2,1,0:T(8,128)S(1)} %bitcast.16) | data formatting | bytes 262144
  59.1 0.6 copy.6
  (1 shorter events, 0.0 us)
Async XLA Ops:
  0.6 1.0 %copy-start = (f32[5,64,128]{2,1,0:T(8,128)S(1)}, f32[5,64,128]{2,1,0:T(8,128)}, u32[]{:S(2)}) copy-start(f32[5,64,128]{2,1,0:T(8,128)} %gate_ref.1) | copy-start | bytes 491524

commit v2 on v1

v2 whole, which is shorter than its diff:
```python
import functools

import jax
import jax.numpy as jnp
from jax import lax
from jax.experimental import pallas as pl
from jax.experimental.pallas import tpu as pltpu
from jax.sharding import PartitionSpec as P

F32 = jnp.float32
BF16 = jnp.bfloat16
MESH = pl.DeviceIdType.MESH
LOCAL_BITS = 14
FIRST = (8, 0, 4, 1, 7)
ORDER = (2, 0, 5, 1, 4, 3)
ROWS = (7, 8, 13, 10, 11, 12, 9)
LANES = (0, 1, 2, 3, 4, 5, 6)
ROWS_MIXED = (7, 8, 13, 4, 5, 6, 9)
NN = (((1,), (0,)), ((), ()))
NT = (((1,), (1,)), ((), ()))
TN = (((0,), (0,)), ((), ()))


def target_bits(layer):
    return [(FIRST[layer] + ORDER[(j + layer) % 6]) % LOCAL_BITS for j in range(6)]


def mm(a, b, dims):
    return lax.dot_general(a, b, dims, preferred_element_type=F32)


def halves(x):
    top = x.astype(BF16)
    return top, (x - top.astype(F32)).astype(BF16)


def mm3(a, b, dims):
    return mm(a[0], b[0], dims) + mm(a[0], b[1], dims) + mm(a[1], b[0], dims)


def gate_code(index, layer, bits):
    code = None
    for j, target in enumerate(target_bits(layer)):
        term = ((index >> bits.index(target)) & 1) << j
        code = term if code is None else code + term
    return code


def rest_position(layer, bits):
    targets = target_bits(layer)
    return [i for i, bit in enumerate(bits) if bit not in targets][0]


def picks(layer, bits):
    row = lax.broadcasted_iota(jnp.int32, (256, 128), 0)
    column = lax.broadcasted_iota(jnp.int32, (256, 128), 1)
    code = gate_code(row & 127, layer, bits) + ((row >> 7) << 6)
    return (code == column).astype(F32).astype(BF16)


def rest_mask(layer, bits):
    i = lax.broadcasted_iota(jnp.int32, (128, 128), 0)
    j = lax.broadcasted_iota(jnp.int32, (128, 128), 1)
    return (((i ^ j) >> rest_position(layer, bits)) & 1) == 0


def spread_gate(u, layer, bits, picked, mask, on_rows):
    row = lax.broadcasted_iota(jnp.int32, (128, 64), 0)
    column = lax.broadcasted_iota(jnp.int32, (128, 64), 1)
    chooser = (gate_code(row, layer, bits) == column).astype(F32).astype(BF16)
    u_parts = halves(u)
    tall = jnp.concatenate([mm(chooser, part, NN).astype(BF16) for part in u_parts], 0)
    out = []
    if on_rows:
        wide = mm(picked, tall, NT)
        for part in range(2):
            columns = slice(128 * part, 128 * part + 128)
            real = jnp.where(mask, wide[:128, columns], 0.0)
            imag = jnp.where(mask, wide[128:, columns], 0.0)
            out.append(jnp.concatenate([jnp.concatenate([real, imag], 1), jnp.concatenate([-imag, real], 1)], 0).astype(BF16))
    else:
        wide = mm(tall, picked, NT)
        for part in range(2):
            rows = slice(128 * part, 128 * part + 128)
            real = jnp.where(mask, wide[rows, :128], 0.0)
            imag = jnp.where(mask, wide[rows, 128:], 0.0)
            out.append(jnp.concatenate([jnp.concatenate([real, -imag], 1), jnp.concatenate([imag, real], 1)], 0).astype(BF16))
    return tuple(out)


def undo_on_rows(gate, x):
    flat = jnp.concatenate([jnp.concatenate([x[0], x[2]], 1), jnp.concatenate([x[1], x[3]], 1)], 0)
    y = mm3(gate, halves(flat), NN)
    return [y[:128, :128], y[128:, :128], y[:128, 128:], y[128:, 128:]]


def undo_on_lanes(gate, x):
    flat = jnp.concatenate([jnp.concatenate([x[0], x[1]], 1), jnp.concatenate([x[2], x[3]], 1)], 0)
    y = mm3(halves(flat), gate, NN)
    return [y[:128, :128], y[:128, 128:], y[128:, :128], y[128:, 128:]]


def outer_on_rows(bra, ket):
    left = jnp.concatenate(bra, 1)
    right = jnp.concatenate([jnp.concatenate([ket[0], ket[1]], 1), jnp.concatenate([ket[1], -ket[0]], 1)], 0)
    return mm3(halves(left), halves(right), NT)


def outer_on_lanes(bra, ket):
    left = jnp.concatenate(bra, 0)
    right = jnp.concatenate([jnp.concatenate([ket[0], ket[1]], 1), jnp.concatenate([ket[1], -ket[0]], 1)], 0)
    return mm3(halves(left), halves(right), TN)


def to_chunks(wide, layer, bits, picked, mask, slot, by_plane):
    kept = jnp.concatenate([jnp.where(mask, wide[:, :128], 0.0), jnp.where(mask, wide[:, 128:], 0.0)], 1)
    both = mm(jnp.concatenate(halves(kept), 0), picked, NN)
    narrow = jnp.concatenate(halves(both[:128] + both[128:]), 0)
    shape = (256 if by_plane else 64, 256)
    row = lax.broadcasted_iota(jnp.int32, shape, 0)
    column = lax.broadcasted_iota(jnp.int32, shape, 1)
    code = gate_code(column & 127, layer, bits)
    if by_plane:
        place = (((code & 15) ^ 1) << 4) + ((code >> 5) << 3) + (((code >> 4) & 1) << 2) + slot
    else:
        place = (((code & 7) ^ 1) << 3) + (code >> 3)
    return mm((row == place).astype(F32).astype(BF16), narrow, NN)


def swap_lane(x, row_bit, lane_bit):
    size, step = 1 << row_bit, 1 << lane_bit
    lane = lax.broadcasted_iota(jnp.int32, (size, 128), 1)
    upper = ((lane >> lane_bit) & 1) == 1
    out = []
    for base in range(0, 128, 2 * size):
        a, b = x[base : base + size], x[base + size : base + 2 * size]
        out.append(jnp.where(upper, pltpu.roll(b, step, 1), a))
        out.append(jnp.where(upper, b, pltpu.roll(a, 128 - step, 1)))
    return jnp.concatenate(out, 0)


def swap_sublane(x, row_bit):
    upper = lax.broadcasted_iota(jnp.int32, (8, 128), 0) >= 4
    tiles = [x[8 * i : 8 * i + 8] for i in range(16)]
    bit = 1 << (row_bit - 3)
    out = [None] * 16
    for i in range(16):
        if not i & bit:
            a, b = tiles[i], tiles[i | bit]
            out[i] = jnp.where(upper, pltpu.roll(b, 4, 0), a)
            out[i | bit] = jnp.where(upper, b, pltpu.roll(a, 4, 0))
    return jnp.concatenate(out, 0)


def hops(k):
    in_y = 1 if k & 1 else (2 if k & 16 else 0)
    in_x = 1 if k & 4 else (2 if k & 8 else 0)
    return 2 * (in_x + in_y) + ((k >> 1) & 1)


IN_PLANE = sorted(range(1, 32), key=hops, reverse=True)
IN_LINE = [k >> 1 for k in IN_PLANE if k < 16 and not k & 1]


def kernel(
    scale, ket_ref, bra_ref, gate_hbm, outs,
    states, gates, send_a, recv_a, send_b, recv_b, chunks, partial, packed, column,
    line_out, line_in, rows_out, rows_in, extra, share, final,
    in_sem, a_send, a_recv, b_send, b_recv, c_send, c_recv, z_send, z_recv, l_send, l_recv, q_send, q_recv, f_send, f_recv, line, near, mid, far,
):
    hi, lo = lax.axis_index("hi"), lax.axis_index("lo")
    z, y = lo & 31, lo >> 5
    me = hi * 2 + y
    loads = [
        pltpu.make_async_copy(gate_hbm, gates, in_sem.at[2]),
        pltpu.make_async_copy(ket_ref, states.at[0], in_sem.at[0]),
        pltpu.make_async_copy(bra_ref, states.at[1], in_sem.at[1]),
    ]
    for load in loads:
        load.start()

    def ring(step):
        return (hi, (lo & 32) + ((z + step) & 31))

    def in_plane(k):
        return (hi ^ (k >> 1), lo ^ ((k & 1) * 32))

    barrier = pltpu.get_barrier_semaphore()

    def greet(device):
        pl.semaphore_signal(barrier, inc=1, device_id=device, device_id_type=MESH)

    for step in (2, -2, 1, -1):
        greet(ring(step))
    for k in IN_LINE:
        greet((hi ^ k, lo))
    for k in (16, 17, 1):
        greet(in_plane(k))
    extra[...] = jnp.zeros((2, 8, 128), F32)
    loads[0].wait()

    def layer_setup(layer, bits, on_rows):
        picked, mask = picks(layer, bits), rest_mask(layer, bits)
        return picked, mask, spread_gate(gates[layer], layer, bits, picked, mask, on_rows)

    pick4, mask4, gate4 = layer_setup(4, ROWS, True)
    pick3, mask3, gate3 = layer_setup(3, LANES, False)

    loads[1].wait()
    loads[2].wait()
    x5 = [swap_sublane(states[s, pl.ds(c, 128, stride=2), :], 6) for s in range(2) for c in range(2)]
    x4 = undo_on_rows(gate4, x5)
    x3 = undo_on_lanes(gate3, x4)
    mine = ((hi >> 2) & 1) * 2 + ((lo >> 1) & 1)
    for i in range(4):
        ready = swap_lane(x3[i], 5, 3)
        for block in range(4):
            send_a[block, i] = ready[32 * block : 32 * block + 32]

    pl.semaphore_wait(barrier, 14)

    def copy_a(d):
        return pltpu.make_async_remote_copy(
            send_a.at[mine ^ d], recv_a.at[mine], a_send.at[d], a_recv.at[d],
            device_id=(hi ^ (4 if d & 2 else 0), lo ^ (2 if d & 1 else 0)), device_id_type=MESH,
        )

    copy_a(1).start()
    copy_a(2).start()
    for k in IN_LINE:
        pl.semaphore_signal(line, inc=1, device_id=(hi ^ k, lo), device_id_type=MESH)
    for step in (2, -2):
        pl.semaphore_signal(near, inc=1, device_id=ring(step), device_id_type=MESH)
    recv_a[mine] = send_a[mine]

    def all_of(ref, sem):
        pltpu.make_async_copy(ref, ref, sem).wait()

    first = to_chunks(outer_on_rows(x5[2:], x4[:2]), 4, ROWS, pick4, mask4, 0, True)
    first += to_chunks(outer_on_lanes(x4[2:], x3[:2]), 3, LANES, pick3, mask3, 3, True)
    chunks[...] = first.reshape(32, 8, 128)
    partial[me] = chunks[me]
    pl.semaphore_wait(line, 7)
    copy_a(3).start()
    pl.semaphore_wait(near, 2)
    for step in (4, -4):
        pl.semaphore_signal(mid, inc=1, device_id=ring(step), device_id_type=MESH)
    for k in IN_PLANE:
        pltpu.make_async_remote_copy(
            chunks.at[me ^ k], partial.at[me], c_send, c_recv, device_id=in_plane(k), device_id_type=MESH,
        ).start()

    pick2, mask2, gate2 = layer_setup(2, ROWS_MIXED, True)
    pick1, mask1, gate1 = layer_setup(1, LANES, False)
    pick0, mask0, gate0 = layer_setup(0, ROWS, True)
    pl.semaphore_wait(mid, 2)
    for step in (8, -8):
        pl.semaphore_signal(far, inc=1, device_id=ring(step), device_id_type=MESH)

    for d in (1, 2, 3):
        copy_a(d).wait()
    x = [jnp.concatenate([recv_a[block, i] for block in range(4)], 0) for i in range(4)]
    x = [swap_lane(v, 5, 3) for v in x]
    mixed = [swap_lane(swap_lane(swap_lane(v, 3, 4), 4, 5), 5, 6) for v in x]

    def send_line(layer, value):
        line_out[layer] = value.reshape(8, 8, 128)
        for k in IN_LINE:
            pltpu.make_async_remote_copy(
                line_out.at[layer, (hi & 7) ^ k], line_in.at[layer, hi & 7], l_send.at[layer], l_recv.at[layer],
                device_id=(hi ^ k, lo), device_id_type=MESH,
            ).start()
        line_in[layer, hi & 7] = line_out[layer, hi & 7]

    x2 = undo_on_rows(gate2, mixed)
    turned = [swap_lane(swap_lane(swap_lane(v, 3, 4), 4, 5), 5, 6) for v in x2]
    x1 = undo_on_lanes(gate1, turned)
    send_line(2, to_chunks(outer_on_rows(mixed[2:], x2[:2]), 2, ROWS_MIXED, pick2, mask2, 0, False))
    x0 = undo_on_rows(gate0, x1)
    send_line(1, to_chunks(outer_on_lanes(turned[2:], x1[:2]), 1, LANES, pick1, mask1, 0, False))
    send_line(0, to_chunks(outer_on_rows(x1[2:], x0[:2]), 0, ROWS, pick0, mask0, 0, False))

    own = ((hi >> 1) & 1) * 4 + (lo & 1) * 2 + (hi & 1)
    for i in range(4):
        ready = swap_sublane(swap_lane(swap_lane(x0[i], 5, 6), 4, 0), 3)
        for block in range(8):
            for top in range(2):
                send_b[block, i, top] = ready[64 * top + 8 * block : 64 * top + 8 * block + 8]
    recv_b[own] = send_b[own]
    copies_b = []
    for d in range(1, 8):
        copy = pltpu.make_async_remote_copy(
            send_b.at[own ^ d], recv_b.at[own], b_send.at[d], b_recv.at[d],
            device_id=(hi ^ ((2 if d & 4 else 0) + (d & 1)), lo ^ (1 if d & 2 else 0)), device_id_type=MESH,
        )
        copy.start()
        copies_b.append(copy)

    sub = lax.broadcasted_iota(jnp.int32, (8, 128), 0)
    all_of(partial.at[pl.ds(0, 31)], c_recv)
    sum1 = jnp.sum(partial[...], 0)
    turned1 = pltpu.roll(sum1, 4, 0)
    for q in range(2):
        three, four = (turned1, sum1) if q else (sum1, turned1)
        packed[q] = jnp.where(sub == 3, three, jnp.where(sub == 4, four, 0.0))
    pl.semaphore_wait(far, 2)

    def column_copy(q):
        return pltpu.make_async_remote_copy(
            packed.at[q], column.at[z], z_send.at[q], z_recv,
            device_id=(hi, (lo & 32) + (hi ^ 1) + 16 * q), device_id_type=MESH,
        )

    sums = []
    for layer in (2, 1, 0):
        all_of(line_in.at[layer, pl.ds(0, 7)], l_recv.at[layer])
        sums.insert(0, jnp.sum(line_in[layer], 0))
    for q in range(4):
        value = jnp.zeros((8, 128), F32)
        for layer in range(3):
            shift = (layer - q) % 8
            value = jnp.where(sub & 3 == layer, pltpu.roll(sums[layer], shift, 0) if shift else sums[layer], value)
        rows_out[q] = value

    def row_copy(q):
        return pltpu.make_async_remote_copy(
            rows_out.at[q], rows_in.at[z], q_send.at[q], q_recv,
            device_id=(hi, (lo & 32) + ((hi & 7) ^ 1) + 8 * q), device_id_type=MESH,
        )

    for q in range(4):
        @pl.when(z != ((hi & 7) ^ 1) + 8 * q)
        def _():
            row_copy(q).start()

        @pl.when(z == ((hi & 7) ^ 1) + 8 * q)
        def _():
            rows_in[z] = rows_out[q]

    for q in range(2):
        @pl.when(z != (hi ^ 1) + 16 * q)
        def _():
            column_copy(q).start()

        @pl.when(z == (hi ^ 1) + 16 * q)
        def _():
            column[z] = packed[q]

    for copy in copies_b:
        copy.wait()
    for i in range(4):
        v = jnp.concatenate([recv_b[block, i, top] for top in range(2) for block in range(8)], 0)
        v = swap_lane(swap_lane(swap_sublane(v, 3), 4, 0), 5, 6)
        outs[pl.ds(256 * (i // 2) + i % 2, 128, stride=2), :] = swap_sublane(v, 6)
    all_of(chunks.at[pl.ds(0, 31)], c_send)
    for layer in range(3):
        all_of(line_out.at[layer, pl.ds(0, 7)], l_send.at[layer])
    for q in range(2):
        @pl.when(z != (hi ^ 1) + 16 * q)
        def _():
            column_copy(q).wait_send()

    for q in range(4):
        @pl.when(z != ((hi & 7) ^ 1) + 8 * q)
        def _():
            row_copy(q).wait_send()

    sink = ((z ^ hi) & 7) == 1
    slot = (hi >> 3) * 2 + y

    @pl.when(z & 15 == (hi ^ 1))
    def _():
        all_of(column.at[pl.ds(0, 31)], z_recv)
        extra[y] = jnp.sum(column[...], 0)

    @pl.when(sink)
    def _():
        all_of(rows_in.at[pl.ds(0, 31)], q_recv)
        total = jnp.sum(rows_in[...], 0)
        share[0] = jnp.where(sub < 3, total, 0.0) + extra[0]
        share[1] = jnp.where(sub < 3, pltpu.roll(total, 4, 0), 0.0) + extra[1]
        for k in IN_PLANE:
            pltpu.make_async_remote_copy(
                share.at[y ^ (k & 1)], final.at[slot], f_send, f_recv, device_id=in_plane(k), device_id_type=MESH,
            ).start()
        final[slot] = share[y]
        all_of(final.at[pl.ds(0, 3)], f_recv)

    @pl.when(jnp.logical_not(sink))
    def _():
        all_of(final.at[pl.ds(0, 4)], f_recv)

    outs[512:520, :] = jnp.sum(final[...], 0) * scale
    @pl.when(sink)
    def _():
        all_of(column.at[pl.ds(0, 31)], f_send)


def body(ket_state, bra_state, gate_matrices):
    scale = (64 / (16384 * lax.axis_size("hi") * lax.axis_size("lo"))) ** 0.5
    amplitudes = ket_state.shape[1]
    hbm = pl.BlockSpec(memory_space=pltpu.HBM)
    dma = pltpu.SemaphoreType.DMA
    regular = pltpu.SemaphoreType.REGULAR
    whole = pl.pallas_call(
        functools.partial(kernel, scale),
        out_shape=jax.ShapeDtypeStruct((520, 128), F32),
        in_specs=[hbm] * 3,
        out_specs=pl.BlockSpec(memory_space=pltpu.VMEM),
        scratch_shapes=[
            pltpu.VMEM((2, 256, 128), F32),
            pltpu.VMEM((5, 64, 128), F32),
            pltpu.VMEM((4, 4, 32, 128), F32),
            pltpu.VMEM((4, 4, 32, 128), F32),
            pltpu.VMEM((8, 4, 2, 8, 128), F32),
            pltpu.VMEM((8, 4, 2, 8, 128), F32),
            pltpu.VMEM((32, 8, 128), F32),
            pltpu.VMEM((32, 8, 128), F32),
            pltpu.VMEM((2, 8, 128), F32),
            pltpu.VMEM((32, 8, 128), F32),
            pltpu.VMEM((3, 8, 8, 128), F32),
            pltpu.VMEM((3, 8, 8, 128), F32),
            pltpu.VMEM((4, 8, 128), F32),
            pltpu.VMEM((32, 8, 128), F32),
            pltpu.VMEM((2, 8, 128), F32),
            pltpu.VMEM((2, 8, 128), F32),
            pltpu.VMEM((4, 8, 128), F32),
            dma((3,)), dma((4,)), dma((4,)), dma((8,)), dma((8,)),
            dma, dma, dma((2,)), dma, dma((3,)), dma((3,)), dma((4,)), dma, dma, dma,
            regular, regular, regular, regular,
        ],
        compiler_params=pltpu.CompilerParams(collective_id=0, has_side_effects=True, vmem_limit_bytes=40 * 2**20),
        name="window",
    )(
        *(
            pltpu.with_memory_space_constraint(v, pltpu.HBM)
            for v in (
                ket_state.reshape(2, 128, 128).transpose(1, 0, 2).reshape(256, 128),
                bra_state.reshape(2, 128, 128).transpose(1, 0, 2).reshape(256, 128),
                gate_matrices,
            )
        ),
    )
    ket, bra = (v.reshape(128, 2, 128).transpose(1, 0, 2).reshape(2, amplitudes) for v in (whole[:256], whole[256:512]))
    return ket, bra, whole[512:517].reshape(5, 1, 128)


def solution(mesh):
    placed = (P(None, ("hi", "lo")), P(None, ("hi", "lo")), P())
    return jax.shard_map(
        body,
        mesh=mesh,
        in_specs=placed,
        out_specs=(P(None, ("hi", "lo")), P(None, ("hi", "lo")), P(None, "lo", None)),
        check_vma=False,
    )
```

time: 60.2 us -> 55.1 us (0.915)
  Pallas kernels: 55.9 us -> 53 us
  local copies, waits for them, and re-layouts: 3.13 us -> 1.3 us
    pallas_call x1, Pallas kernels: 55.9 us -> 53 us  [body(): pl.pallas_call(functools.partial(kernel, scale), out_shape=jax.ShapeDtype...]
    unnamed x5 -> x1, local copies, waits for them, and re-layouts: 2.11 us -> 0.58 us
    reshape x2 -> x1, local copies, waits for them, and re-layouts: 1.02 us -> 0.01 us  [body(): return (ket, bra, whole[512:517].reshape(5, 1, 128))]
    slice x0 -> x1, local copies, waits for them, and re-layouts: none -> 0.72 us  [body(): whole[256:512]]
where the time goes in v2:
time: 55.1 us; the launch traced here: 55 us
  Pallas kernels  53 us (96%)
  local copies, waits for them, and re-layouts  1.3 us (2%)
  between operations  0.64 us (1%)
    pallas_call x1, Pallas kernels, body(): pl.pallas_call(functools.partial(kernel, scale), out_shape=jax.ShapeDtype...  53 us

profile of v2, /device:TPU:1, one launch (start us, length us, event | category | flops | bytes accessed | tf_op | source)
XLA Modules:
  0.0 55.0 jit_solution(4763467317587246394)
XLA Ops:
  0.6 53.0 %window.1 = f32[520,128]{1,0:T(8,128)S(1)} custom-call(f32[256,128]{1,0:T(8,128)} %bitcast.22, f32[256,128]{1,0:T(8,128)} %bitcast.23, f32[5,64,128]{2,1,0:T(8,128)} %gate_hbm.1), custom_call_target="tpu_custom_call" | custom-call | tf_op jit(solution)/shard_map/window/pallas_call | solution.py:405
  53.7 0.7 %fusion = (f32[256,128]{1,0:T(8,128)}, f32[256,128]{1,0:T(8,128)}) fusion(f32[520,128]{1,0:T(8,128)S(1)} %window.1), kind=kLoop, calls=%fused_computation.1 | loop fusion | bytes 524288 | tf_op jit(solution)/shard_map/slice | solution.py:444
  54.4 0.6 %copy.10 = f32[5,1,128]{2,1,0:T(1,128)} copy(f32[5,1,128]{2,0,1:T(8,128)S(1)} %slice_bitcast_fusion) | data formatting | bytes 5120
  (1 shorter events, 0.0 us)

commit v3 on v2

--- a/solution.py
+++ b/solution.py
@@ -49,6 +49,10 @@
 def rest_position(layer, bits):
     targets = target_bits(layer)
     return [i for i, bit in enumerate(bits) if bit not in targets][0]
+
+
+def holder(z):
+    return ((z & 3) << 1) + 1 - (z >> 2)
 
 
 def picks(layer, bits):
@@ -121,9 +125,9 @@
     column = lax.broadcasted_iota(jnp.int32, shape, 1)
     code = gate_code(column & 127, layer, bits)
     if by_plane:
-        place = (((code & 15) ^ 1) << 4) + ((code >> 5) << 3) + (((code >> 4) & 1) << 2) + slot
+        place = (((code & 8) + holder(code & 7)) << 4) + ((code >> 5) << 3) + (((code >> 4) & 1) << 2) + slot
     else:
-        place = (((code & 7) ^ 1) << 3) + (code >> 3)
+        place = (holder(code & 7) << 3) + (code >> 3)
     return mm((row == place).astype(F32).astype(BF16), narrow, NN)
 
 
@@ -171,6 +175,7 @@
     hi, lo = lax.axis_index("hi"), lax.axis_index("lo")
     z, y = lo & 31, lo >> 5
     me = hi * 2 + y
+    held = ((hi & 7) >> 1) + ((1 - (hi & 1)) << 2)
     loads = [
         pltpu.make_async_copy(gate_hbm, gates, in_sem.at[2]),
         pltpu.make_async_copy(ket_ref, states.at[0], in_sem.at[0]),
@@ -190,6 +195,7 @@
     def greet(device):
         pl.semaphore_signal(barrier, inc=1, device_id=device, device_id_type=MESH)
 
+    greet((hi ^ 4, lo ^ 2))
     for step in (2, -2, 1, -1):
         greet(ring(step))
     for k in IN_LINE:
@@ -217,7 +223,7 @@
         for block in range(4):
             send_a[block, i] = ready[32 * block : 32 * block + 32]
 
-    pl.semaphore_wait(barrier, 14)
+    pl.semaphore_wait(barrier, 15)
 
     def copy_a(d):
         return pltpu.make_async_remote_copy(
@@ -225,6 +231,7 @@
             device_id=(hi ^ (4 if d & 2 else 0), lo ^ (2 if d & 1 else 0)), device_id_type=MESH,
         )
 
+    copy_a(3).start()
     copy_a(1).start()
     copy_a(2).start()
     for k in IN_LINE:
@@ -241,7 +248,6 @@
     chunks[...] = first.reshape(32, 8, 128)
     partial[me] = chunks[me]
     pl.semaphore_wait(line, 7)
-    copy_a(3).start()
     pl.semaphore_wait(near, 2)
     for step in (4, -4):
         pl.semaphore_signal(mid, inc=1, device_id=ring(step), device_id_type=MESH)
@@ -308,7 +314,7 @@
     def column_copy(q):
         return pltpu.make_async_remote_copy(
             packed.at[q], column.at[z], z_send.at[q], z_recv,
-            device_id=(hi, (lo & 32) + (hi ^ 1) + 16 * q), device_id_type=MESH,
+            device_id=(hi, (lo & 32) + held + (hi & 8) + 16 * q), device_id_type=MESH,
         )
 
     sums = []
@@ -325,24 +331,24 @@
     def row_copy(q):
         return pltpu.make_async_remote_copy(
             rows_out.at[q], rows_in.at[z], q_send.at[q], q_recv,
-            device_id=(hi, (lo & 32) + ((hi & 7) ^ 1) + 8 * q), device_id_type=MESH,
+            device_id=(hi, (lo & 32) + held + 8 * q), device_id_type=MESH,
         )
 
     for q in range(4):
-        @pl.when(z != ((hi & 7) ^ 1) + 8 * q)
+        @pl.when(z != held + 8 * q)
         def _():
             row_copy(q).start()
 
-        @pl.when(z == ((hi & 7) ^ 1) + 8 * q)
+        @pl.when(z == held + 8 * q)
         def _():
             rows_in[z] = rows_out[q]
 
     for q in range(2):
-        @pl.when(z != (hi ^ 1) + 16 * q)
+        @pl.when(z != held + (hi & 8) + 16 * q)
         def _():
             column_copy(q).start()
 
-        @pl.when(z == (hi ^ 1) + 16 * q)
+        @pl.when(z == held + (hi & 8) + 16 * q)
         def _():
             column[z] = packed[q]
 
@@ -356,19 +362,19 @@
     for layer in range(3):
         all_of(line_out.at[layer, pl.ds(0, 7)], l_send.at[layer])
     for q in range(2):
-        @pl.when(z != (hi ^ 1) + 16 * q)
+        @pl.when(z != held + (hi & 8) + 16 * q)
         def _():
             column_copy(q).wait_send()
 
     for q in range(4):
-        @pl.when(z != ((hi & 7) ^ 1) + 8 * q)
+        @pl.when(z != held + 8 * q)
         def _():
             row_copy(q).wait_send()
 
-    sink = ((z ^ hi) & 7) == 1
+    sink = (z & 7) == held
     slot = (hi >> 3) * 2 + y
 
-    @pl.when(z & 15 == (hi ^ 1))
+    @pl.when((z & 15) == held + (hi & 8))
     def _():
         all_of(column.at[pl.ds(0, 31)], z_recv)
         extra[y] = jnp.sum(column[...], 0)
@@ -394,6 +400,20 @@
     @pl.when(sink)
     def _():
         all_of(column.at[pl.ds(0, 31)], f_send)
+
+
+def put_kernel(whole, ket, bra, grad, slim, sem):
+    copies = [
+        pltpu.make_async_copy(whole.at[pl.ds(0, 256)], ket, sem.at[0]),
+        pltpu.make_async_copy(whole.at[pl.ds(256, 256)], bra, sem.at[1]),
+        pltpu.make_async_copy(slim, grad, sem.at[2]),
+    ]
+    for layer in range(5):
+        slim[layer] = whole[512 + layer : 513 + layer, :]
+    for copy in copies:
+        copy.start()
+    for copy in copies:
+        copy.wait()
 
 
 def body(ket_state, bra_state, gate_matrices):
@@ -441,8 +461,18 @@
             )
         ),
     )
-    ket, bra = (v.reshape(128, 2, 128).transpose(1, 0, 2).reshape(2, amplitudes) for v in (whole[:256], whole[256:512]))
-    return ket, bra, whole[512:517].reshape(5, 1, 128)
+    state = jax.ShapeDtypeStruct((256, 128), F32)
+    slim = jax.ShapeDtypeStruct((5, 1, 128), F32)
+    ket, bra, grad = pl.pallas_call(
+        put_kernel,
+        out_shape=(state, state, slim),
+        in_specs=[pl.BlockSpec(memory_space=pltpu.VMEM)],
+        out_specs=(hbm,) * 3,
+        scratch_shapes=[pltpu.VMEM((5, 1, 128), F32), dma((3,))],
+        name="put",
+    )(pltpu.with_memory_space_constraint(whole, pltpu.VMEM))
+    ket, bra = (v.reshape(128, 2, 128).transpose(1, 0, 2).reshape(2, amplitudes) for v in (ket, bra))
+    return ket, bra, grad
 
 
 def solution(mesh):

time: 55.1 us -> 53.7 us (0.975)
  local copies, waits for them, and re-layouts: 1.3 us -> 0 us
    pallas_call x1, Pallas kernels: 53 us -> 52.2 us  [body(): pl.pallas_call(functools.partial(kernel, scale), out_shape=jax.ShapeDtype...]
    pallas_call x0 -> x1, Pallas kernels: none -> 0.73 us  [body(): pl.pallas_call(put_kernel, out_shape=(state, state, slim), in_specs=[pl.B...]
    slice x1 -> x0, local copies, waits for them, and re-layouts: 0.72 us -> none  [body(): whole[256:512]]
    unnamed x1 -> x0, local copies, waits for them, and re-layouts: 0.58 us -> none
where the time goes in v3:
time: 53.7 us; the launch traced here: 53.5 us
  Pallas kernels  52.9 us (99%)
  between operations  0.64 us (1%)
    pallas_call x1, Pallas kernels, body(): pl.pallas_call(functools.partial(kernel, scale), out_shape=jax.ShapeDtype...  52.2 us

profile of v3, /device:TPU:1, one launch (start us, length us, event | category | flops | bytes accessed | tf_op | source)
XLA Modules:
  0.0 53.5 jit_solution(299557342840668593)
XLA Ops:
  0.6 52.2 %window.1.whole = f32[520,128]{1,0:T(8,128)S(1)} custom-call(f32[256,128]{1,0:T(8,128)} %bitcast.20, f32[256,128]{1,0:T(8,128)} %bitcast.21, f32[5,64,128]{2,1,0:T(8,128)} %gate_hbm.1), custom_call_target="tpu_custom_call" | custom-call | tf_op jit(solution)/shard_map/window/pallas_call | solution.py:425
  52.8 0.7 %put.1 = (f32[256,128]{1,0:T(8,128)}, f32[256,128]{1,0:T(8,128)}, f32[5,1,128]{2,1,0:T(1,128)}) custom-call(f32[520,128]{1,0:T(8,128)S(1)} %window.1.whole), custom_call_target="tpu_custom_call" | custom-call | tf_op jit(solution)/shard_map/put/pallas_call | solution.py:466

commit v4 on v3

--- a/solution.py
+++ b/solution.py
@@ -225,15 +225,16 @@
 
     pl.semaphore_wait(barrier, 15)
 
-    def copy_a(d):
+    def copy_a(d, s):
+        both = pl.ds(2 * s, 2)
         return pltpu.make_async_remote_copy(
-            send_a.at[mine ^ d], recv_a.at[mine], a_send.at[d], a_recv.at[d],
+            send_a.at[mine ^ d, both], recv_a.at[mine, both], a_send.at[s, d], a_recv.at[s, d],
             device_id=(hi ^ (4 if d & 2 else 0), lo ^ (2 if d & 1 else 0)), device_id_type=MESH,
         )
 
-    copy_a(3).start()
-    copy_a(1).start()
-    copy_a(2).start()
+    for s in range(2):
+        for d in (3, 1, 2):
+            copy_a(d, s).start()
     for k in IN_LINE:
         pl.semaphore_signal(line, inc=1, device_id=(hi ^ k, lo), device_id_type=MESH)
     for step in (2, -2):
@@ -263,11 +264,22 @@
     for step in (8, -8):
         pl.semaphore_signal(far, inc=1, device_id=ring(step), device_id_type=MESH)
 
-    for d in (1, 2, 3):
-        copy_a(d).wait()
-    x = [jnp.concatenate([recv_a[block, i] for block in range(4)], 0) for i in range(4)]
-    x = [swap_lane(v, 5, 3) for v in x]
-    mixed = [swap_lane(swap_lane(swap_lane(v, 3, 4), 4, 5), 5, 6) for v in x]
+    def arrived(s):
+        for d in (3, 1, 2):
+            copy_a(d, s).wait()
+        x = [jnp.concatenate([recv_a[block, 2 * s + c] for block in range(4)], 0) for c in range(2)]
+        return turn([swap_lane(v, 5, 3) for v in x])
+
+    def turn(x):
+        return [swap_lane(swap_lane(swap_lane(v, 3, 4), 4, 5), 5, 6) for v in x]
+
+    def one_on_rows(gate, x):
+        out = mm3(gate, halves(jnp.concatenate(x, 0)), NN)
+        return [out[:128], out[128:]]
+
+    def one_on_lanes(gate, x):
+        out = mm3(halves(jnp.concatenate(x, 1)), gate, NN)
+        return [out[:, :128], out[:, 128:]]
 
     def send_line(layer, value):
         line_out[layer] = value.reshape(8, 8, 128)
@@ -278,13 +290,16 @@
             ).start()
         line_in[layer, hi & 7] = line_out[layer, hi & 7]
 
-    x2 = undo_on_rows(gate2, mixed)
-    turned = [swap_lane(swap_lane(swap_lane(v, 3, 4), 4, 5), 5, 6) for v in x2]
-    x1 = undo_on_lanes(gate1, turned)
-    send_line(2, to_chunks(outer_on_rows(mixed[2:], x2[:2]), 2, ROWS_MIXED, pick2, mask2, 0, False))
-    x0 = undo_on_rows(gate0, x1)
-    send_line(1, to_chunks(outer_on_lanes(turned[2:], x1[:2]), 1, LANES, pick1, mask1, 0, False))
-    send_line(0, to_chunks(outer_on_rows(x1[2:], x0[:2]), 0, ROWS, pick0, mask0, 0, False))
+    ket2 = one_on_rows(gate2, arrived(0))
+    ket1 = one_on_lanes(gate1, turn(ket2))
+    ket0 = one_on_rows(gate0, ket1)
+    bra3 = arrived(1)
+    send_line(2, to_chunks(outer_on_rows(bra3, ket2), 2, ROWS_MIXED, pick2, mask2, 0, False))
+    bra2 = turn(one_on_rows(gate2, bra3))
+    send_line(1, to_chunks(outer_on_lanes(bra2, ket1), 1, LANES, pick1, mask1, 0, False))
+    bra1 = one_on_lanes(gate1, bra2)
+    send_line(0, to_chunks(outer_on_rows(bra1, ket0), 0, ROWS, pick0, mask0, 0, False))
+    x0 = ket0 + one_on_rows(gate0, bra1)
 
     own = ((hi >> 1) & 1) * 4 + (lo & 1) * 2 + (hi & 1)
     for i in range(4):
@@ -445,7 +460,7 @@
             pltpu.VMEM((2, 8, 128), F32),
             pltpu.VMEM((2, 8, 128), F32),
             pltpu.VMEM((4, 8, 128), F32),
-            dma((3,)), dma((4,)), dma((4,)), dma((8,)), dma((8,)),
+            dma((3,)), dma((2, 4)), dma((2, 4)), dma((8,)), dma((8,)),
             dma, dma, dma((2,)), dma, dma((3,)), dma((3,)), dma((4,)), dma, dma, dma,
             regular, regular, regular, regular,
         ],

time: 53.7 us -> 54.3 us (1.011)
  Pallas kernels: 52.9 us -> 53.5 us
    pallas_call x1, Pallas kernels: 52.2 us -> 52.8 us  [body(): pl.pallas_call(functools.partial(kernel, scale), out_shape=jax.ShapeDtype...]
where the time goes in v4:
time: 54.3 us; the launch traced here: 54.2 us
  Pallas kernels  53.5 us (99%)
  between operations  0.64 us (1%)
    pallas_call x1, Pallas kernels, body(): pl.pallas_call(functools.partial(kernel, scale), out_shape=jax.ShapeDtype...  52.8 us

profile of v4, /device:TPU:1, one launch (start us, length us, event | category | flops | bytes accessed | tf_op | source)
XLA Modules:
  0.0 54.2 jit_solution(18057107534855689031)
XLA Ops:
  0.6 52.8 %window.1.whole = f32[520,128]{1,0:T(8,128)S(1)} custom-call(f32[256,128]{1,0:T(8,128)} %bitcast.20, f32[256,128]{1,0:T(8,128)} %bitcast.21, f32[5,64,128]{2,1,0:T(8,128)} %gate_hbm.1), custom_call_target="tpu_custom_call" | custom-call | tf_op jit(solution)/shard_map/window/pallas_call | solution.py:440
  53.5 0.7 %put.1 = (f32[256,128]{1,0:T(8,128)}, f32[256,128]{1,0:T(8,128)}, f32[5,1,128]{2,1,0:T(1,128)}) custom-call(f32[520,128]{1,0:T(8,128)S(1)} %window.1.whole), custom_call_target="tpu_custom_call" | custom-call | tf_op jit(solution)/shard_map/put/pallas_call | solution.py:481

commit v5 on v3

--- a/solution.py
+++ b/solution.py
@@ -231,8 +231,8 @@
             device_id=(hi ^ (4 if d & 2 else 0), lo ^ (2 if d & 1 else 0)), device_id_type=MESH,
         )
 
+    copy_a(1).start()
     copy_a(3).start()
-    copy_a(1).start()
     copy_a(2).start()
     for k in IN_LINE:
         pl.semaphore_signal(line, inc=1, device_id=(hi ^ k, lo), device_id_type=MESH)

time: 53.7 us -> 54.3 us (1.011)
  Pallas kernels: 52.9 us -> 53.5 us
    pallas_call x1, Pallas kernels: 52.2 us -> 52.8 us  [body(): pl.pallas_call(functools.partial(kernel, scale), out_shape=jax.ShapeDtype...]
where the time goes in v5:
time: 54.3 us; the launch traced here: 54.1 us
  Pallas kernels  53.5 us (99%)
  between operations  0.64 us (1%)
    pallas_call x1, Pallas kernels, body(): pl.pallas_call(functools.partial(kernel, scale), out_shape=jax.ShapeDtype...  52.8 us

profile of v5, /device:TPU:1, one launch (start us, length us, event | category | flops | bytes accessed | tf_op | source)
XLA Modules:
  0.0 54.1 jit_solution(17326756392934740566)
XLA Ops:
  0.6 52.8 %window.1.whole = f32[520,128]{1,0:T(8,128)S(1)} custom-call(f32[256,128]{1,0:T(8,128)} %bitcast.20, f32[256,128]{1,0:T(8,128)} %bitcast.21, f32[5,64,128]{2,1,0:T(8,128)} %gate_hbm.1), custom_call_target="tpu_custom_call" | custom-call | tf_op jit(solution)/shard_map/window/pallas_call | solution.py:425
  53.4 0.7 %put.1 = (f32[256,128]{1,0:T(8,128)}, f32[256,128]{1,0:T(8,128)}, f32[5,1,128]{2,1,0:T(1,128)}) custom-call(f32[520,128]{1,0:T(8,128)S(1)} %window.1.whole), custom_call_target="tpu_custom_call" | custom-call | tf_op jit(solution)/shard_map/put/pallas_call | solution.py:466
